TPU v7x, 32 devices: a whole 2x2x4 slice. The times are simulated.
32 devices in a mesh: dp: 2 (over core), seq: 16 (over z, y, x).
Axes of the slice: x: 2, y: 2, z: 4, core: 2. Of those that a mesh axis runs over, the one named last changes fastest.
Arguments:
- query: bfloat16 [2, 2048, 512], P('dp', 'seq'), may hold values from -6 to 6
- key_in: bfloat16 [2, 2048, 128], P('dp', 'seq'), may hold values from -4.5 to 4.5
- value_in: bfloat16 [2, 2048, 128], P('dp', 'seq'), may hold values from -6 to 6
- out_gain: float32 [512], replicated, may hold values from 0.1 to 1.9
- cotangent: bfloat16 [2, 2048, 512], P('dp', 'seq'), may hold values from -6 to 6
Outputs:
- attended: bfloat16 [2, 2048, 512], P('dp', 'seq')
- grad_query: bfloat16 [2, 2048, 512], P('dp', 'seq')
- grad_key: bfloat16 [2, 2048, 128], P('dp', 'seq')
- grad_value: bfloat16 [2, 2048, 128], P('dp', 'seq')
- grad_gain: float32 [512], replicated
All inputs are finite; a program needn't handle non-finite values.
Results may differ from a plain program's by a relative error of at most 0.012.
The roundings to bfloat16 on the way count: a program that leaves them out, or rounds other values in their place, can miss the bound.
Values may be sent and summed in bfloat16 or wider, within the bound.
A program may use at most 128 MiB of HBM per device.

v0:
```python
import math

import jax
import jax.numpy as jnp
from jax import lax
from jax.sharding import PartitionSpec as P

HEADS = 4
KEY = 128
VAL = 128


def to_rows(tokens, heads):
    positions = tokens.shape[0]
    width = tokens.shape[1] // heads
    return (
        tokens.reshape(positions, heads, width).transpose(1, 0, 2).reshape(heads * positions, width)
    )


def to_tokens(rows_in, heads):
    positions = rows_in.shape[0] // heads
    width = rows_in.shape[1]
    return (
        rows_in.reshape(heads, positions, width)
        .transpose(1, 0, 2)
        .reshape(positions, heads * width)
    )


def contract_first(left_mat, right_mat):
    return lax.dot_general(
        left_mat, right_mat, (((0,), (0,)), ((), ())), preferred_element_type=jnp.float32
    )


def contract_last(left_mat, right_mat):
    return lax.dot_general(
        left_mat, right_mat, (((1,), (1,)), ((), ())), preferred_element_type=jnp.float32
    )


def body(query, key_in, value_in, out_gain, cotangent):
    keys_all, values_all = (
        lax.all_gather(key_in, "seq", axis=1, tiled=True),
        lax.all_gather(value_in, "seq", axis=1, tiled=True),
    )
    key_mat = keys_all[0]
    value_mat = values_all[0]
    length = key_mat.shape[0]
    positions = query.shape[1]
    shards = lax.axis_size("seq")
    score_scale = 1.0 / math.sqrt(KEY)
    query_rows = to_rows(query[0], HEADS)
    scores = contract_last(query_rows, key_mat) * score_scale
    row_top = jnp.max(scores, axis=1, keepdims=True)
    expo_rows = jnp.exp(scores - row_top)
    weights = (expo_rows / jnp.sum(expo_rows, axis=1, keepdims=True)).astype(jnp.bfloat16)
    out_rows = jnp.dot(weights, value_mat, preferred_element_type=jnp.float32)
    out_tokens = to_tokens(out_rows, HEADS)
    attended = (out_tokens * out_gain).astype(jnp.bfloat16)
    upstream = cotangent[0].astype(jnp.float32)
    gain_total = lax.psum(jnp.sum(upstream * out_tokens, axis=0), ("dp", "seq"))
    token_total = lax.axis_size("dp") * shards * positions
    grad_gain = gain_total / math.sqrt(token_total)
    grad_out = (upstream * out_gain).astype(jnp.bfloat16)
    grad_rows = to_rows(grad_out, HEADS)
    delta_rows = jnp.sum(grad_rows.astype(jnp.float32) * out_rows, axis=1, keepdims=True)
    block_size = 2048
    block_starts = jnp.arange(length // block_size, dtype=jnp.int32) * block_size
    query_zero = jnp.zeros((query_rows.shape[0], KEY), jnp.float32)

    def score_grad(offset_at):
        key_part = lax.dynamic_slice_in_dim(key_mat, offset_at, block_size, 0)
        value_part = lax.dynamic_slice_in_dim(value_mat, offset_at, block_size, 0)
        weight_part = lax.dynamic_slice_in_dim(weights, offset_at, block_size, 1)
        d_prob = contract_last(grad_rows, value_part)
        d_score = (weight_part.astype(jnp.float32) * (d_prob - delta_rows)).astype(jnp.bfloat16)
        return (d_score, key_part, weight_part)

    def advance_both(query_acc, offset_at):
        d_score, key_part, weight_part = score_grad(offset_at)
        query_acc = query_acc + jnp.dot(d_score, key_part, preferred_element_type=jnp.float32)
        key_term = contract_first(d_score, query_rows) * score_scale
        value_term = contract_first(weight_part, grad_rows)
        return (query_acc, (key_term, value_term))

    query_acc, both_terms = lax.scan(advance_both, query_zero, block_starts)
    key_recv, value_recv = (
        lax.all_to_all(
            both_terms[0].reshape(shards, positions, KEY),
            "seq",
            split_axis=0,
            concat_axis=0,
            tiled=True,
        ),
        lax.all_to_all(
            both_terms[1].reshape(shards, positions, VAL),
            "seq",
            split_axis=0,
            concat_axis=0,
            tiled=True,
        ),
    )
    grad_key = jnp.sum(key_recv, axis=0)
    grad_value = jnp.sum(value_recv, axis=0)
    grad_query = to_tokens(query_acc * score_scale, HEADS).astype(jnp.bfloat16)
    return (
        attended[None],
        grad_query[None],
        grad_key.astype(jnp.bfloat16)[None],
        grad_value.astype(jnp.bfloat16)[None],
        grad_gain,
    )


def solution(mesh):
    placed = (
        P("dp", "seq", None),
        P("dp", "seq", None),
        P("dp", "seq", None),
        P(),
        P("dp", "seq", None),
    )
    return jax.shard_map(
        body,
        mesh=mesh,
        in_specs=placed,
        out_specs=(
            P("dp", "seq", None),
            P("dp", "seq", None),
            P("dp", "seq", None),
            P("dp", "seq", None),
            P(),
        ),
        check_vma=False,
    )
```

profile of v0, /device:TPU:0, one launch (start us, length us, event | category | flops | bytes accessed | tf_op | source)
XLA Modules:
  0.0 178.8 jit_solution(7083140095282552283)
XLA Ops:
  0.6 1.0 reshape.112
  1.6 1.0 copy.20
  2.7 0.1 copy.21
  2.8 45.6 %all_gather.6 = bf16[1,2048,128]{2,1,0:T(8,128)(2,1)S(1)} all-gather(bf16[1,128,128]{2,1,0:T(8,128)(2,1)} %param.6), channel_id=1, replica_groups=mesh['dp'=2,'seq'=16] {'seq'}, dimensions={1}, use_global_device_ids=true | all-gather | bytes 557056 | tf_op jit(solution)/shard_map/all_gather | solution.py:45
  48.4 0.0 copy-start.1
  48.4 0.8 copy-done.1
  49.1 0.8 multiply_reduce_fusion
  49.9 0.0 copy-start
  49.9 0.8 fusion
  50.7 0.0 copy-start.2
  50.8 0.0 copy-start.3
  50.8 0.8 divide_convert_fusion
  51.6 0.2 copy-done
  51.9 0.0 copy-done.2
  51.9 39.0 %all_gather.7 = bf16[1,2048,128]{2,1,0:T(8,128)(2,1)S(1)} all-gather(bf16[1,128,128]{2,1,0:T(8,128)(2,1)S(1)} %copy-done.2), channel_id=1, replica_groups=mesh['dp'=2,'seq'=16] {'seq'}, dimensions={1}, use_global_device_ids=true | all-gather | bytes 557056 | tf_op jit(solution)/shard_map/all_gather | solution.py:46
  90.9 0.0 copy-done.3
  90.9 0.7 multiply_reduce_fusion.1
  91.6 0.2 multiply_reduce_fusion.2
  91.8 0.7 multiply_convert_fusion
  92.5 1.8 convolution_multiply_fusion
  94.3 4.2 %all-to-all-start = ((f32[16,128,128]{2,1,0:T(8,128)}), f32[16,128,128]{2,1,0:T(8,128)S(1)}, u32[]{:S(2)}, u32[]{:S(2)}) async-start(f32[16,128,128]{2,1,0:T(8,128)} %bitcast.13), calls=%async_computation | async-start | bytes 2097152 | tf_op jit(solution)/shard_map/all_to_all | solution.py:90
  98.5 4.4 %fusion.17 = bf16[2048,512]{0,1:T(8,128)(2,1)} fusion(f32[512]{0:T(512)S(1)} %fusion, f32[512]{0:T(512)S(1)} %get-tuple-element.27, f32[512,2048]{1,0:T(8,128)} %copy-done), kind=kLoop, calls=%fused_computation.22 | loop fusion | flops 4194304 | bytes 6295552 | tf_op jit(solution)/shard_map/div | solution.py:58
  102.9 3.9 %copy.27 = bf16[2048,512]{1,0:T(8,128)(2,1)} copy(bf16[2048,512]{0,1:T(8,128)(2,1)} %fusion.17) | data formatting | bytes 4194304 | tf_op jit(solution)/shard_map/while/body/eval_jaxpr/dot_general | solution.py:32
  106.8 3.3 %fusion.8 = f32[16,128,128]{2,1,0:T(8,128)} fusion(bf16[16,128,512]{2,1,0:T(8,128)(2,1)} %bitcast.51, bf16[512,128,1]{1,0,2:T(8,128)(2,1)S(1)} %bitcast.54), kind=kOutput, calls=%fused_computation.21 | convolution fusion | flops 268435456 | bytes 3276800 | tf_op jit(solution)/shard_map/while/body/eval_jaxpr/dot_general | solution.py:32
  110.1 11.1 %all-to-all-done = f32[16,128,128]{2,1,0:T(8,128)S(1)} async-done(((f32[16,128,128]{2,1,0:T(8,128)}), f32[16,128,128]{2,1,0:T(8,128)S(1)}, u32[]{:S(2)}, u32[]{:S(2)}) %all-to-all-start) | async-done | bytes 1048608 | tf_op jit(solution)/shard_map/all_to_all | solution.py:90
  121.2 8.2 %all-to-all-start.1 = ((f32[16,128,128]{2,1,0:T(8,128)}), f32[16,128,128]{2,1,0:T(8,128)}, u32[]{:S(2)}, u32[]{:S(2)}) async-start(f32[16,128,128]{2,1,0:T(8,128)} %fusion.8), calls=%async_computation.1 | async-start | bytes 2097152 | tf_op jit(solution)/shard_map/all_to_all | solution.py:97
  129.4 0.9 copy.22
  130.2 1.1 reshape.109
  131.3 1.7 fusion.1
  133.1 0.1 copy.24
  133.2 0.7 convert_element_type.93
  133.9 41.1 %psum.7 = f32[512]{0:T(512)S(1)} all-reduce(f32[512]{0:T(512)S(1)} %bitcast.62), channel_id=1, replica_groups=mesh['dp'=2,'seq'=16] {'dp','seq'}, use_global_device_ids=true, to_apply=%region_6.7 | all-reduce | flops 512 | bytes 4096 | tf_op jit(solution)/shard_map/psum | solution.py:63
  174.9 0.6 broadcast_multiply_fusion
  175.5 0.7 multiply_convert_fusion.2
  176.2 0.7 reduce_sum.49
  176.9 0.0 all-to-all-done.1
  176.9 1.9 %reduce_sum.50 = bf16[128,128]{1,0:T(8,128)(2,1)} reduce(f32[16,128,128]{2,1,0:T(8,128)} %all-to-all-done.1, f32[]{:T(128)} %constant.10.clone.1), dimensions={0}, to_apply=%region_4.0 | reduce | flops 245760 | bytes 1081348 | tf_op jit(solution)/shard_map/reduce_sum | solution.py:106
Async XLA Ops:
  48.4 0.8 copy-start.1
  49.9 1.9 %copy-start = (f32[512,2048]{1,0:T(8,128)}, f32[512,2048]{1,0:T(8,128)S(1)}, u32[]{:S(2)}) copy-start(f32[512,2048]{1,0:T(8,128)S(1)} %get-tuple-element.28) | copy-start | bytes 12582916
  50.7 1.1 copy-start.2
  50.8 40.2 %copy-start.3 = (f32[512]{0:T(512)S(1)}, f32[512]{0:T(512)}, u32[]{:S(2)}) copy-start(f32[512]{0:T(512)} %param.8) | copy-start | bytes 6148
  94.3 26.9 %all-to-all-start = ((f32[16,128,128]{2,1,0:T(8,128)}), f32[16,128,128]{2,1,0:T(8,128)S(1)}, u32[]{:S(2)}, u32[]{:S(2)}) async-start(f32[16,128,128]{2,1,0:T(8,128)} %bitcast.13), calls=%async_computation | async-start | bytes 2097152 | tf_op jit(solution)/shard_map/all_to_all | solution.py:90
  121.2 55.7 %all-to-all-start.1 = ((f32[16,128,128]{2,1,0:T(8,128)}), f32[16,128,128]{2,1,0:T(8,128)}, u32[]{:S(2)}, u32[]{:S(2)}) async-start(f32[16,128,128]{2,1,0:T(8,128)} %fusion.8), calls=%async_computation.1 | async-start | bytes 2097152 | tf_op jit(solution)/shard_map/all_to_all | solution.py:97
where the time goes:
time: 180 us; the launch traced here: 179 us
  blocking collectives  126 us (70%)
  starting transfers between devices  12.4 us (7%)
  waiting for transfers between devices  11.1 us (6%)
  other arithmetic  10 us (6%)
  local copies, waits for them, and re-layouts  9.87 us (5%)
  matrix products  9.01 us (5%)
    all_gather x1, blocking collectives, body(): lax.all_gather(key_in, 'seq', axis=1, tiled=True)  45.6 us
    psum x1, blocking collectives, body(): gain_total = lax.psum(jnp.sum(upstream * out_tokens, axis=0), ('dp', 'seq'))  41.1 us
    all_gather x1, blocking collectives, body(): lax.all_gather(value_in, 'seq', axis=1, tiled=True)  39 us
    all_to_all x1, waiting for transfers between devices, body(): lax.all_to_all(both_terms[0].reshape(shards, positions, KEY), 'seq', spli...  11.1 us
    all_to_all x1, starting transfers between devices, body(): lax.all_to_all(both_terms[1].reshape(shards, positions, VAL), 'seq', spli...  8.16 us
    dot_general x2, matrix products, contract_first(): lax.dot_general(left_mat, right_mat, (((0,), (0,)), ((), ())), preferred_...  5.03 us
    div x1, other arithmetic, body(): expo_rows / jnp.sum(expo_rows, axis=1, keepdims=True)  4.36 us
    all_to_all x1, starting transfers between devices, body(): lax.all_to_all(both_terms[0].reshape(shards, positions, KEY), 'seq', spli...  4.22 us
  transfers between devices with their start and end apart: 2, of which 1 were waited for; matrix products, arithmetic and copies ran while one was open for 10% of the time, Pallas kernels for 0%

commit v1 on v0

--- a/solution.py
+++ b/solution.py
@@ -3,6 +3,8 @@
 import jax
 import jax.numpy as jnp
 from jax import lax
+from jax.experimental import pallas as pl
+from jax.experimental.pallas import tpu as pltpu
 from jax.sharding import PartitionSpec as P
 
 HEADS = 4
@@ -114,6 +116,307 @@
     )
 
 
+BF = jnp.bfloat16
+F32 = jnp.float32
+DEPTH = 4
+SIDE = 2
+SLOTS = DEPTH * SIDE * SIDE
+COPIES = 80
+
+
+def fused_kernel(
+    q_ref, k_ref, v_ref, gain_ref, cot_ref,
+    att_ref, gq_ref, gk_ref, gv_ref, gg_ref,
+    kbuf, vbuf, qbuf, cbuf, qrows, grows, gtrans, ebuf, dpbuf, pbuf, dsbuf,
+    ksend, vsend, kown, vown, kfirst, ksecond, kthird, vfirst, vsecond, vthird,
+    gsend, grecv, local_sem, send_sem, recv_sem,
+):
+    dp = lax.axis_index("dp")
+    me = lax.axis_index("seq")
+    x = me % 2
+    y = (me // 2) % 2
+    z = me // 4
+    other_core = (1 - dp, me)
+    x_peer = (dp, me + 1 - 2 * x)
+    y_peer = (dp, me + 2 - 4 * y)
+    low = me % 4
+    z_peers = {
+        1: (dp, (z + 1 - 2 * (z % 2)) * 4 + low),
+        2: (dp, ((z + 2) % 4) * 4 + low),
+        3: (dp, (3 - z) * 4 + low),
+    }
+
+    def local(src, dst, index):
+        copy = pltpu.make_async_copy(src, dst, local_sem.at[index])
+        copy.start()
+        return copy
+
+    k_local = local(k_ref.at[0], kbuf.at[0], 0)
+    v_local = local(v_ref.at[0], vbuf.at[0], 1)
+    q_local = local(q_ref.at[0], qbuf, 2)
+    c_local = local(cot_ref.at[0], cbuf, 3)
+
+    barrier = pltpu.get_barrier_semaphore()
+    peers = [other_core, x_peer, y_peer] + [z_peers[d] for d in (1, 2, 3)]
+    for peer in peers:
+        pl.semaphore_signal(barrier, inc=1, device_id=peer, device_id_type=pl.DeviceIdType.MESH)
+    pl.semaphore_wait(barrier, len(peers))
+
+    sent = []
+
+    def send(src, dst, peer):
+        index = len(sent)
+        copy = pltpu.make_async_remote_copy(
+            src_ref=src, dst_ref=dst, send_sem=send_sem.at[index], recv_sem=recv_sem.at[index],
+            device_id=peer, device_id_type=pl.DeviceIdType.MESH,
+        )
+        copy.start()
+        sent.append(copy)
+        return copy
+
+    k_in, v_in = {}, {}
+    k_local.wait()
+    for d in (1, 2, 3):
+        k_in[4 * d] = send(kbuf.at[0], kbuf.at[4 * d], z_peers[d])
+    k_in[1] = send(kbuf.at[0], kbuf.at[1], x_peer)
+    v_local.wait()
+    v_in[2] = send(vbuf.at[0], vbuf.at[2], y_peer)
+    for d in (1, 2, 3):
+        v_in[4 * d] = send(vbuf.at[0], vbuf.at[4 * d], z_peers[d])
+    k_in[2] = send(kbuf.at[0], kbuf.at[2], y_peer)
+    v_in[1] = send(vbuf.at[0], vbuf.at[1], x_peer)
+
+    positions = qbuf.shape[0]
+    gain = gain_ref[...]
+    q_local.wait()
+    c_local.wait()
+    for h in range(HEADS):
+        lanes = slice(h * KEY, (h + 1) * KEY)
+        rows = slice(h * positions, (h + 1) * positions)
+        qrows[rows, :] = qbuf[:, lanes]
+        out_grad = (cbuf[:, lanes].astype(F32) * gain[:, lanes]).astype(BF)
+        grows[rows, :] = out_grad
+        gtrans[:, rows] = out_grad.astype(F32).T
+
+    rate = math.log2(math.e) / math.sqrt(KEY)
+    score_scale = 1.0 / math.sqrt(KEY)
+    tops, sums = {}, {}
+
+    def score(r):
+        raw = contract_last(kbuf[r], qrows[...])
+        top = jnp.max(raw, axis=0, keepdims=True)
+        expo = jnp.exp2((raw - top) * rate)
+        tops[r] = top
+        sums[r] = jnp.sum(expo, axis=0, keepdims=True)
+        ebuf[r] = expo
+
+    def d_prob(r):
+        dpbuf[r] = contract_last(vbuf[r], grows[...])
+
+    score(0)
+    d_prob(0)
+    for d in range(4):
+        base = 4 * d
+        if d:
+            k_in[base].wait_recv()
+            k_in[base + 1] = send(kbuf.at[base], kbuf.at[base + 1], x_peer)
+            k_in[base + 2] = send(kbuf.at[base], kbuf.at[base + 2], y_peer)
+            v_in[base].wait_recv()
+            v_in[base + 2] = send(vbuf.at[base], vbuf.at[base + 2], y_peer)
+            v_in[base + 1] = send(vbuf.at[base], vbuf.at[base + 1], x_peer)
+            score(base)
+            d_prob(base)
+        if d != 1:
+            done = [0] if d == 0 else [d - 1] if d > 2 else [1]
+            for e in done:
+                at = 4 * e
+                k_in[at + 1].wait_recv()
+                k_in[at + 3] = send(kbuf.at[at + 1], kbuf.at[at + 3], y_peer)
+                v_in[at + 2].wait_recv()
+                v_in[at + 3] = send(vbuf.at[at + 2], vbuf.at[at + 3], x_peer)
+                score(at + 1)
+                d_prob(at + 2)
+    k_in[13].wait_recv()
+    k_in[15] = send(kbuf.at[13], kbuf.at[15], y_peer)
+    v_in[14].wait_recv()
+    v_in[15] = send(vbuf.at[14], vbuf.at[15], x_peer)
+    score(13)
+    d_prob(14)
+    for d in range(4):
+        k_in[4 * d + 2].wait_recv()
+        score(4 * d + 2)
+        v_in[4 * d + 1].wait_recv()
+        d_prob(4 * d + 1)
+    for d in range(4):
+        k_in[4 * d + 3].wait_recv()
+        score(4 * d + 3)
+        v_in[4 * d + 3].wait_recv()
+        d_prob(4 * d + 3)
+
+    top_all = tops[0]
+    for r in range(1, SLOTS):
+        top_all = jnp.maximum(top_all, tops[r])
+    factors = [jnp.exp2((tops[r] - top_all) * rate) for r in range(SLOTS)]
+    total = sums[0] * factors[0]
+    for r in range(1, SLOTS):
+        total = total + sums[r] * factors[r]
+    inverse = 1.0 / total
+    out_t = None
+    for r in range(SLOTS):
+        weight = (ebuf[r] * (factors[r] * inverse)).astype(BF)
+        pbuf[r] = weight
+        term = jnp.dot(vbuf[r].T, weight, preferred_element_type=F32)
+        out_t = term if out_t is None else out_t + term
+    delta = jnp.sum(gtrans[...] * out_t, axis=0, keepdims=True)
+
+    k_first, k_second, k_third, v_first, v_second, v_third = {}, {}, {}, {}, {}, {}
+
+    def terms(r):
+        weight = pbuf[r]
+        d_score = (weight.astype(F32) * (dpbuf[r] - delta)).astype(BF)
+        dsbuf[r] = d_score
+        key_term = jnp.dot(d_score, qrows[...], preferred_element_type=F32) * score_scale
+        value_term = jnp.dot(weight, grows[...], preferred_element_type=F32)
+        return key_term, value_term
+
+    for d in (3, 2, 1, 0):
+        r = 4 * d + 3
+        key_term, value_term = terms(r)
+        ksend[r] = key_term.astype(BF)
+        vsend[r] = value_term.astype(BF)
+        k_first[d, 1] = send(ksend.at[r], kfirst.at[2 * d + 1], y_peer)
+        v_first[d, 1] = send(vsend.at[r], vfirst.at[2 * d + 1], x_peer)
+    for d in (3, 2, 1, 0):
+        r = 4 * d + 2
+        key_term, value_term = terms(r)
+        ksend[r] = key_term.astype(BF)
+        k_first[d, 0] = send(ksend.at[r], kfirst.at[2 * d], y_peer)
+        vown[2 * d + 1] = value_term
+        r = 4 * d + 1
+        key_term, value_term = terms(r)
+        vsend[r] = value_term.astype(BF)
+        v_first[d, 0] = send(vsend.at[r], vfirst.at[2 * d], x_peer)
+        kown[2 * d + 1] = key_term
+
+    gain_terms = []
+    for h in range(HEADS):
+        lanes = slice(h * VAL, (h + 1) * VAL)
+        out_h = out_t[:, h * positions : (h + 1) * positions].T
+        att_ref[0, :, lanes] = (out_h * gain[:, lanes]).astype(BF)
+        gain_terms.append(jnp.sum(cbuf[:, lanes].astype(F32) * out_h, axis=0, keepdims=True))
+    gain_sum = jnp.broadcast_to(jnp.concatenate(gain_terms, axis=1), (8, HEADS * VAL))
+    gsend[0] = gain_sum
+    gain_copy = send(gsend.at[0], grecv.at[0], other_core)
+
+    for d in (3, 2, 1, 0):
+        k_first[d, 1].wait_recv()
+        ksend[4 * d + 1] = (kown[2 * d + 1] + kfirst[2 * d + 1].astype(F32)).astype(BF)
+        k_second[d] = send(ksend.at[4 * d + 1], ksecond.at[d], x_peer)
+        v_first[d, 1].wait_recv()
+        vsend[4 * d + 2] = (vown[2 * d + 1] + vfirst[2 * d + 1].astype(F32)).astype(BF)
+        v_second[d] = send(vsend.at[4 * d + 2], vsecond.at[d], y_peer)
+
+    gain_copy.wait_recv()
+    gain_sum = gain_sum + grecv[0]
+    gsend[1] = gain_sum
+    gain_copy = send(gsend.at[1], grecv.at[1], x_peer)
+
+    for d in (3, 2, 1, 0):
+        key_term, value_term = terms(4 * d)
+        kown[2 * d] = key_term
+        vown[2 * d] = value_term
+
+    gain_copy.wait_recv()
+    gain_sum = gain_sum + grecv[1]
+    gsend[2] = gain_sum
+    gain_copy = send(gsend.at[2], grecv.at[2], y_peer)
+
+    query_t = None
+    for r in range(SLOTS):
+        term = jnp.dot(kbuf[r].T, dsbuf[r], preferred_element_type=F32)
+        query_t = term if query_t is None else query_t + term
+    for h in range(HEADS):
+        part = query_t[:, h * positions : (h + 1) * positions] * score_scale
+        gq_ref[0, :, h * KEY : (h + 1) * KEY] = part.T.astype(BF)
+
+    gain_copy.wait_recv()
+    gain_sum = gain_sum + grecv[2]
+    gsend[3] = gain_sum
+    gain_copies = [send(gsend.at[3], grecv.at[2 + d], z_peers[d]) for d in (1, 2, 3)]
+
+    for d in (3, 2, 1, 0):
+        k_first[d, 0].wait_recv()
+        k_second[d].wait_recv()
+        key_sum = kown[2 * d] + kfirst[2 * d].astype(F32) + ksecond[d].astype(F32)
+        v_first[d, 0].wait_recv()
+        v_second[d].wait_recv()
+        value_sum = vown[2 * d] + vfirst[2 * d].astype(F32) + vsecond[d].astype(F32)
+        if d:
+            ksend[4 * d] = key_sum.astype(BF)
+            k_third[d] = send(ksend.at[4 * d], kthird.at[d - 1], z_peers[d])
+            vsend[4 * d] = value_sum.astype(BF)
+            v_third[d] = send(vsend.at[4 * d], vthird.at[d - 1], z_peers[d])
+
+    for copy in gain_copies:
+        copy.wait_recv()
+    gain_sum = (gain_sum + grecv[3]) + (grecv[4] + grecv[5])
+    token_total = lax.axis_size("dp") * lax.axis_size("seq") * positions
+    gg_ref[...] = gain_sum[0:1, :] / math.sqrt(token_total)
+
+    for d in (3, 2, 1):
+        k_third[d].wait_recv()
+        key_sum = key_sum + kthird[d - 1].astype(F32)
+        v_third[d].wait_recv()
+        value_sum = value_sum + vthird[d - 1].astype(F32)
+    gk_ref[0] = key_sum.astype(BF)
+    gv_ref[0] = value_sum.astype(BF)
+    for copy in sent:
+        copy.wait_send()
+
+
+def fused_body(query, key_in, value_in, out_gain, cotangent):
+    positions = query.shape[1]
+    rows = HEADS * positions
+    any_space = pl.BlockSpec(memory_space=pl.ANY)
+    vmem = pl.BlockSpec(memory_space=pltpu.VMEM)
+    key_slot = lambda count, kind: pltpu.VMEM((count, positions, KEY), kind)
+    scratch = [
+        key_slot(SLOTS, BF), key_slot(SLOTS, BF),
+        pltpu.VMEM((positions, HEADS * KEY), BF), pltpu.VMEM((positions, HEADS * VAL), BF),
+        pltpu.VMEM((rows, KEY), BF), pltpu.VMEM((rows, VAL), BF), pltpu.VMEM((VAL, rows), F32),
+        pltpu.VMEM((SLOTS, positions, rows), F32), pltpu.VMEM((SLOTS, positions, rows), F32),
+        pltpu.VMEM((SLOTS, positions, rows), BF), pltpu.VMEM((SLOTS, positions, rows), BF),
+        key_slot(SLOTS, BF), key_slot(SLOTS, BF),
+        key_slot(8, F32), key_slot(8, F32),
+        key_slot(8, BF), key_slot(4, BF), key_slot(3, BF),
+        key_slot(8, BF), key_slot(4, BF), key_slot(3, BF),
+        pltpu.VMEM((4, 8, HEADS * VAL), F32), pltpu.VMEM((6, 8, HEADS * VAL), F32),
+        pltpu.SemaphoreType.DMA((4,)), pltpu.SemaphoreType.DMA((COPIES,)), pltpu.SemaphoreType.DMA((COPIES,)),
+    ]
+    outs = pl.pallas_call(
+        fused_kernel,
+        out_shape=[
+            jax.ShapeDtypeStruct(query.shape, BF),
+            jax.ShapeDtypeStruct(query.shape, BF),
+            jax.ShapeDtypeStruct(key_in.shape, BF),
+            jax.ShapeDtypeStruct(value_in.shape, BF),
+            jax.ShapeDtypeStruct((1, HEADS * VAL), F32),
+        ],
+        in_specs=[any_space, any_space, any_space, vmem, any_space],
+        out_specs=[vmem] * 5,
+        scratch_shapes=scratch,
+        compiler_params=pltpu.CompilerParams(
+            collective_id=0, has_side_effects=True, vmem_limit_bytes=48 * 1024 * 1024
+        ),
+        cost_estimate=pl.CostEstimate(
+            flops=12 * rows * SLOTS * positions * KEY,
+            bytes_accessed=8 * positions * HEADS * KEY,
+            transcendentals=rows * SLOTS * positions,
+        ),
+    )(query, key_in, value_in, out_gain.reshape(1, -1), cotangent)
+    return (*outs[:4], outs[4].reshape(-1))
+
+
 def solution(mesh):
     placed = (
         P("dp", "seq", None),
@@ -122,8 +425,9 @@
         P(),
         P("dp", "seq", None),
     )
+    fits = mesh.shape["seq"] == SLOTS and mesh.shape["dp"] == 2
     return jax.shard_map(
-        body,
+        fused_body if fits else body,
         mesh=mesh,
         in_specs=placed,
         out_specs=(

time: 180 us -> 49.3 us (0.27)
  blocking collectives: 126 us -> 0 us
  Pallas kernels: 0 us -> 41.2 us
  starting transfers between devices: 12.4 us -> 0 us
  waiting for transfers between devices: 11.1 us -> 0 us
  other arithmetic: 10 us -> 0 us
  matrix products: 9.01 us -> 0 us
  local copies, waits for them, and re-layouts: 9.87 us -> 7.12 us
    all_gather x2 -> x0, blocking collectives: 84.6 us -> none  [the longest x1 45.6 us: body(): lax.all_gather(key_in, 'seq', axis=1, tiled=True)]
    pallas_call x0 -> x1, Pallas kernels: none -> 41.2 us  [fused_body(): pl.pallas_call(fused_kernel, out_shape=[jax.ShapeDtypeStruct(query.shape,...]
    psum x1 -> x0, blocking collectives: 41.1 us -> none  [body(): gain_total = lax.psum(jnp.sum(upstream * out_tokens, axis=0), ('dp', 'seq'))]
    all_to_all x2 -> x0, starting transfers between devices: 12.4 us -> none  [the longest x1 8.16 us: body(): lax.all_to_all(both_terms[1].reshape(shards, positions, VAL), 'seq', spli...]
    all_to_all x2 -> x0, waiting for transfers between devices: 11.1 us -> none  [the longest x1 11.1 us: body(): lax.all_to_all(both_terms[0].reshape(shards, positions, KEY), 'seq', spli...]
    dot_general x6 -> x0, matrix products: 9.01 us -> none  [the longest x2 5.03 us: contract_first(): lax.dot_general(left_mat, right_mat, (((0,), (0,)), ((), ())), preferred_...]
    unnamed x9 -> x15, local copies, waits for them, and re-layouts: 2.05 us -> 7.12 us
    div x2 -> x0, other arithmetic: 4.94 us -> none  [the longest x1 4.36 us: body(): expo_rows / jnp.sum(expo_rows, axis=1, keepdims=True)]
  transfers between devices with their start and end apart: 2 -> 0, of which waited for: 1 -> 0; matrix products, arithmetic and copies ran while one was open for 10% -> 0% of each run, Pallas kernels for 0% -> 0%
where the time goes in v1:
time: 49.3 us; the launch traced here: 49 us
  Pallas kernels  41.2 us (84%)
  local copies, waits for them, and re-layouts  7.12 us (14%)
  between operations  0.66 us (1%)
    pallas_call x1, Pallas kernels, fused_body(): pl.pallas_call(fused_kernel, out_shape=[jax.ShapeDtypeStruct(query.shape,...  41.2 us
    unnamed x15, local copies, waits for them, and re-layouts  7.12 us

profile of v1, /device:TPU:0, one launch (start us, length us, event | category | flops | bytes accessed | tf_op | source)
XLA Modules:
  0.0 49.0 jit_solution(743191681481412431)
XLA Ops:
  0.6 0.0 copy-start
  0.6 0.9 %copy-done = bf16[1,128,512]{2,1,0:T(8,128)(2,1)S(1)} copy-done((bf16[1,128,512]{2,1,0:T(8,128)(2,1)S(1)}, bf16[1,128,512]{2,1,0:T(8,128)(2,1)}, u32[]{:S(2)}) %copy-start) | copy-done | bytes 131096
  1.5 0.0 copy-start.1
  1.5 0.9 %copy-done.1 = bf16[1,128,512]{2,1,0:T(8,128)(2,1)S(1)} copy-done((bf16[1,128,512]{2,1,0:T(8,128)(2,1)S(1)}, bf16[1,128,512]{2,1,0:T(8,128)(2,1)}, u32[]{:S(2)}) %copy-start.1) | copy-done | bytes 131096
  2.4 0.0 copy-start.2
  2.4 0.8 %copy-done.2 = bf16[1,128,128]{2,1,0:T(8,128)(2,1)S(1)} copy-done((bf16[1,128,128]{2,1,0:T(8,128)(2,1)S(1)}, bf16[1,128,128]{2,1,0:T(8,128)(2,1)}, u32[]{:S(2)}) %copy-start.2) | copy-done | bytes 32792
  3.2 0.0 copy-start.3
  3.2 0.8 %copy-done.3 = bf16[1,128,128]{2,1,0:T(8,128)(2,1)S(1)} copy-done((bf16[1,128,128]{2,1,0:T(8,128)(2,1)S(1)}, bf16[1,128,128]{2,1,0:T(8,128)(2,1)}, u32[]{:S(2)}) %copy-start.3) | copy-done | bytes 32792
  4.0 0.0 copy-start.4
  4.0 0.7 %copy-done.4 = f32[512]{0:T(512)S(1)} copy-done((f32[512]{0:T(512)S(1)}, f32[512]{0:T(512)}, u32[]{:S(2)}) %copy-start.4) | copy-done | bytes 2072
  4.6 41.2 %shard_map.92 = (bf16[1,128,512]{2,1,0:T(8,128)(2,1)S(1)}, bf16[1,128,512]{2,1,0:T(8,128)(2,1)S(1)}, bf16[1,128,128]{2,1,0:T(8,128)(2,1)S(1)}, bf16[1,128,128]{2,1,0:T(8,128)(2,1)S(1)}, f32[1,512]{1,0:T(1,128)S(1)}) custom-call(bf16[1,128,512]{2,1,0:T(8,128)(2,1)S(1)} %copy-done, bf16[1,128,128]{2,1,0:T(8,128)(2,1)S(1)} %copy-done.2, ...), custom_call_target="tpu_custom_call" | custom-call | flops 1610612736 | bytes 524288 | tf_op jit(solution)/shard_map/pallas_call | solution.py:396
  45.9 0.7 %copy.15 = bf16[1,128,512]{2,1,0:T(8,128)(2,1)} copy(bf16[1,128,512]{2,1,0:T(8,128)(2,1)S(1)} %get-tuple-element.20) | data formatting | bytes 262144
  46.6 0.7 %copy.16 = bf16[1,128,512]{2,1,0:T(8,128)(2,1)} copy(bf16[1,128,512]{2,1,0:T(8,128)(2,1)S(1)} %get-tuple-element.21) | data formatting | bytes 262144
  47.2 0.6 %copy.17 = bf16[1,128,128]{2,1,0:T(8,128)(2,1)} copy(bf16[1,128,128]{2,1,0:T(8,128)(2,1)S(1)} %get-tuple-element.22) | data formatting | bytes 65536
  47.8 0.6 %copy.18 = bf16[1,128,128]{2,1,0:T(8,128)(2,1)} copy(bf16[1,128,128]{2,1,0:T(8,128)(2,1)S(1)} %get-tuple-element.23) | data formatting | bytes 65536
  48.4 0.6 %copy.19 = f32[512]{0:T(512)} copy(f32[512]{0:T(512)S(1)} %bitcast.2) | data formatting | bytes 4096
Async XLA Ops:
  0.6 0.9 %copy-start = (bf16[1,128,512]{2,1,0:T(8,128)(2,1)S(1)}, bf16[1,128,512]{2,1,0:T(8,128)(2,1)}, u32[]{:S(2)}) copy-start(bf16[1,128,512]{2,1,0:T(8,128)(2,1)} %q_ref.1) | copy-start | bytes 393220
  1.5 0.9 %copy-start.1 = (bf16[1,128,512]{2,1,0:T(8,128)(2,1)S(1)}, bf16[1,128,512]{2,1,0:T(8,128)(2,1)}, u32[]{:S(2)}) copy-start(bf16[1,128,512]{2,1,0:T(8,128)(2,1)} %cot_ref.1) | copy-start | bytes 393220
  2.4 0.8 %copy-start.2 = (bf16[1,128,128]{2,1,0:T(8,128)(2,1)S(1)}, bf16[1,128,128]{2,1,0:T(8,128)(2,1)}, u32[]{:S(2)}) copy-start(bf16[1,128,128]{2,1,0:T(8,128)(2,1)} %k_ref.1) | copy-start | bytes 98308
  3.2 0.8 %copy-start.3 = (bf16[1,128,128]{2,1,0:T(8,128)(2,1)S(1)}, bf16[1,128,128]{2,1,0:T(8,128)(2,1)}, u32[]{:S(2)}) copy-start(bf16[1,128,128]{2,1,0:T(8,128)(2,1)} %v_ref.1) | copy-start | bytes 98308
  4.0 0.7 %copy-start.4 = (f32[512]{0:T(512)S(1)}, f32[512]{0:T(512)}, u32[]{:S(2)}) copy-start(f32[512]{0:T(512)} %param.8) | copy-start | bytes 6148

commit v2 on v1

--- a/solution.py
+++ b/solution.py
@@ -122,6 +122,7 @@
 SIDE = 2
 SLOTS = DEPTH * SIDE * SIDE
 COPIES = 80
+VMEM_BYTES = 60 * 1024 * 1024
 
 
 def fused_kernel(
@@ -129,7 +130,7 @@
     att_ref, gq_ref, gk_ref, gv_ref, gg_ref,
     kbuf, vbuf, qbuf, cbuf, qrows, grows, gtrans, ebuf, dpbuf, pbuf, dsbuf,
     ksend, vsend, kown, vown, kfirst, ksecond, kthird, vfirst, vsecond, vthird,
-    gsend, grecv, local_sem, send_sem, recv_sem,
+    gsend, grecv, abuf, qout, local_sem, send_sem, recv_sem,
 ):
     dp = lax.axis_index("dp")
     me = lax.axis_index("seq")
@@ -176,13 +177,13 @@
 
     k_in, v_in = {}, {}
     k_local.wait()
+    v_local.wait()
     for d in (1, 2, 3):
         k_in[4 * d] = send(kbuf.at[0], kbuf.at[4 * d], z_peers[d])
-    k_in[1] = send(kbuf.at[0], kbuf.at[1], x_peer)
-    v_local.wait()
-    v_in[2] = send(vbuf.at[0], vbuf.at[2], y_peer)
-    for d in (1, 2, 3):
         v_in[4 * d] = send(vbuf.at[0], vbuf.at[4 * d], z_peers[d])
+        if d == 1:
+            k_in[1] = send(kbuf.at[0], kbuf.at[1], x_peer)
+            v_in[2] = send(vbuf.at[0], vbuf.at[2], y_peer)
     k_in[2] = send(kbuf.at[0], kbuf.at[2], y_peer)
     v_in[1] = send(vbuf.at[0], vbuf.at[1], x_peer)
 
@@ -269,6 +270,17 @@
         out_t = term if out_t is None else out_t + term
     delta = jnp.sum(gtrans[...] * out_t, axis=0, keepdims=True)
 
+    gain_terms = []
+    for h in range(HEADS):
+        lanes = slice(h * VAL, (h + 1) * VAL)
+        out_h = out_t[:, h * positions : (h + 1) * positions].T
+        abuf[:, lanes] = (out_h * gain[:, lanes]).astype(BF)
+        gain_terms.append(jnp.sum(cbuf[:, lanes].astype(F32) * out_h, axis=0, keepdims=True))
+    gain_sum = jnp.concatenate(gain_terms, axis=1)
+    gsend[0] = gain_sum
+    gain_copy = send(gsend.at[0], grecv.at[0], other_core)
+    att_out = local(abuf, att_ref.at[0], 4)
+
     k_first, k_second, k_third, v_first, v_second, v_third = {}, {}, {}, {}, {}, {}
 
     def terms(r):
@@ -279,14 +291,13 @@
         value_term = jnp.dot(weight, grows[...], preferred_element_type=F32)
         return key_term, value_term
 
-    for d in (3, 2, 1, 0):
+    def first_stage(d):
         r = 4 * d + 3
         key_term, value_term = terms(r)
         ksend[r] = key_term.astype(BF)
+        k_first[d, 1] = send(ksend.at[r], kfirst.at[2 * d + 1], y_peer)
         vsend[r] = value_term.astype(BF)
-        k_first[d, 1] = send(ksend.at[r], kfirst.at[2 * d + 1], y_peer)
         v_first[d, 1] = send(vsend.at[r], vfirst.at[2 * d + 1], x_peer)
-    for d in (3, 2, 1, 0):
         r = 4 * d + 2
         key_term, value_term = terms(r)
         ksend[r] = key_term.astype(BF)
@@ -297,18 +308,11 @@
         vsend[r] = value_term.astype(BF)
         v_first[d, 0] = send(vsend.at[r], vfirst.at[2 * d], x_peer)
         kown[2 * d + 1] = key_term
-
-    gain_terms = []
-    for h in range(HEADS):
-        lanes = slice(h * VAL, (h + 1) * VAL)
-        out_h = out_t[:, h * positions : (h + 1) * positions].T
-        att_ref[0, :, lanes] = (out_h * gain[:, lanes]).astype(BF)
-        gain_terms.append(jnp.sum(cbuf[:, lanes].astype(F32) * out_h, axis=0, keepdims=True))
-    gain_sum = jnp.broadcast_to(jnp.concatenate(gain_terms, axis=1), (8, HEADS * VAL))
-    gsend[0] = gain_sum
-    gain_copy = send(gsend.at[0], grecv.at[0], other_core)
-
-    for d in (3, 2, 1, 0):
+        key_term, value_term = terms(4 * d)
+        kown[2 * d] = key_term
+        vown[2 * d] = value_term
+
+    def second_stage(d):
         k_first[d, 1].wait_recv()
         ksend[4 * d + 1] = (kown[2 * d + 1] + kfirst[2 * d + 1].astype(F32)).astype(BF)
         k_second[d] = send(ksend.at[4 * d + 1], ksecond.at[d], x_peer)
@@ -316,20 +320,44 @@
         vsend[4 * d + 2] = (vown[2 * d + 1] + vfirst[2 * d + 1].astype(F32)).astype(BF)
         v_second[d] = send(vsend.at[4 * d + 2], vsecond.at[d], y_peer)
 
+    def third_stage(d):
+        k_first[d, 0].wait_recv()
+        k_second[d].wait_recv()
+        key_sum = kown[2 * d] + kfirst[2 * d].astype(F32) + ksecond[d].astype(F32)
+        if d:
+            ksend[4 * d] = key_sum.astype(BF)
+            k_third[d] = send(ksend.at[4 * d], kthird.at[d - 1], z_peers[d])
+        v_first[d, 0].wait_recv()
+        v_second[d].wait_recv()
+        value_sum = vown[2 * d] + vfirst[2 * d].astype(F32) + vsecond[d].astype(F32)
+        if d:
+            vsend[4 * d] = value_sum.astype(BF)
+            v_third[d] = send(vsend.at[4 * d], vthird.at[d - 1], z_peers[d])
+        return key_sum, value_sum
+
+    first_stage(3)
     gain_copy.wait_recv()
     gain_sum = gain_sum + grecv[0]
     gsend[1] = gain_sum
     gain_copy = send(gsend.at[1], grecv.at[1], x_peer)
-
-    for d in (3, 2, 1, 0):
-        key_term, value_term = terms(4 * d)
-        kown[2 * d] = key_term
-        vown[2 * d] = value_term
-
+    first_stage(2)
+    second_stage(3)
+    first_stage(1)
+    second_stage(2)
+    third_stage(3)
     gain_copy.wait_recv()
     gain_sum = gain_sum + grecv[1]
     gsend[2] = gain_sum
     gain_copy = send(gsend.at[2], grecv.at[2], y_peer)
+    first_stage(0)
+    second_stage(1)
+    third_stage(2)
+    second_stage(0)
+    third_stage(1)
+    gain_copy.wait_recv()
+    gain_sum = gain_sum + grecv[2]
+    gsend[3] = gain_sum
+    gain_copies = [send(gsend.at[3], grecv.at[2 + d], z_peers[d]) for d in (1, 2, 3)]
 
     query_t = None
     for r in range(SLOTS):
@@ -337,32 +365,10 @@
         query_t = term if query_t is None else query_t + term
     for h in range(HEADS):
         part = query_t[:, h * positions : (h + 1) * positions] * score_scale
-        gq_ref[0, :, h * KEY : (h + 1) * KEY] = part.T.astype(BF)
-
-    gain_copy.wait_recv()
-    gain_sum = gain_sum + grecv[2]
-    gsend[3] = gain_sum
-    gain_copies = [send(gsend.at[3], grecv.at[2 + d], z_peers[d]) for d in (1, 2, 3)]
-
-    for d in (3, 2, 1, 0):
-        k_first[d, 0].wait_recv()
-        k_second[d].wait_recv()
-        key_sum = kown[2 * d] + kfirst[2 * d].astype(F32) + ksecond[d].astype(F32)
-        v_first[d, 0].wait_recv()
-        v_second[d].wait_recv()
-        value_sum = vown[2 * d] + vfirst[2 * d].astype(F32) + vsecond[d].astype(F32)
-        if d:
-            ksend[4 * d] = key_sum.astype(BF)
-            k_third[d] = send(ksend.at[4 * d], kthird.at[d - 1], z_peers[d])
-            vsend[4 * d] = value_sum.astype(BF)
-            v_third[d] = send(vsend.at[4 * d], vthird.at[d - 1], z_peers[d])
-
-    for copy in gain_copies:
-        copy.wait_recv()
-    gain_sum = (gain_sum + grecv[3]) + (grecv[4] + grecv[5])
-    token_total = lax.axis_size("dp") * lax.axis_size("seq") * positions
-    gg_ref[...] = gain_sum[0:1, :] / math.sqrt(token_total)
-
+        qout[:, h * KEY : (h + 1) * KEY] = part.T.astype(BF)
+    q_out = local(qout, gq_ref.at[0], 5)
+
+    key_sum, value_sum = third_stage(0)
     for d in (3, 2, 1):
         k_third[d].wait_recv()
         key_sum = key_sum + kthird[d - 1].astype(F32)
@@ -370,8 +376,29 @@
         value_sum = value_sum + vthird[d - 1].astype(F32)
     gk_ref[0] = key_sum.astype(BF)
     gv_ref[0] = value_sum.astype(BF)
+    for copy in gain_copies:
+        copy.wait_recv()
+    gain_sum = (gain_sum + grecv[3]) + (grecv[4] + grecv[5])
+    token_total = lax.axis_size("dp") * lax.axis_size("seq") * positions
+    gg_ref[...] = gain_sum / math.sqrt(token_total)
+    att_out.wait()
+    q_out.wait()
     for copy in sent:
         copy.wait_send()
+
+
+def hand_over(*refs):
+    sources, targets, held = refs[:5], refs[5:10], refs[10:15]
+    in_sem, out_sem = refs[15:]
+    reads = [pltpu.make_async_copy(sources[i], held[i], in_sem.at[i]) for i in range(5)]
+    writes = [pltpu.make_async_copy(held[i], targets[i], out_sem.at[i]) for i in range(5)]
+    for copy in reads:
+        copy.start()
+    for read, write in zip(reads, writes):
+        read.wait()
+        write.start()
+    for copy in writes:
+        copy.wait()
 
 
 def fused_body(query, key_in, value_in, out_gain, cotangent):
@@ -390,8 +417,9 @@
         key_slot(8, F32), key_slot(8, F32),
         key_slot(8, BF), key_slot(4, BF), key_slot(3, BF),
         key_slot(8, BF), key_slot(4, BF), key_slot(3, BF),
-        pltpu.VMEM((4, 8, HEADS * VAL), F32), pltpu.VMEM((6, 8, HEADS * VAL), F32),
-        pltpu.SemaphoreType.DMA((4,)), pltpu.SemaphoreType.DMA((COPIES,)), pltpu.SemaphoreType.DMA((COPIES,)),
+        pltpu.VMEM((4, 1, HEADS * VAL), F32), pltpu.VMEM((6, 1, HEADS * VAL), F32),
+        pltpu.VMEM((positions, HEADS * VAL), BF), pltpu.VMEM((positions, HEADS * KEY), BF),
+        pltpu.SemaphoreType.DMA((6,)), pltpu.SemaphoreType.DMA((COPIES,)), pltpu.SemaphoreType.DMA((COPIES,)),
     ]
     outs = pl.pallas_call(
         fused_kernel,
@@ -403,10 +431,10 @@
             jax.ShapeDtypeStruct((1, HEADS * VAL), F32),
         ],
         in_specs=[any_space, any_space, any_space, vmem, any_space],
-        out_specs=[vmem] * 5,
+        out_specs=[any_space, any_space, vmem, vmem, vmem],
         scratch_shapes=scratch,
         compiler_params=pltpu.CompilerParams(
-            collective_id=0, has_side_effects=True, vmem_limit_bytes=48 * 1024 * 1024
+            collective_id=0, has_side_effects=True, vmem_limit_bytes=VMEM_BYTES
         ),
         cost_estimate=pl.CostEstimate(
             flops=12 * rows * SLOTS * positions * KEY,
@@ -414,6 +442,14 @@
             transcendentals=rows * SLOTS * positions,
         ),
     )(query, key_in, value_in, out_gain.reshape(1, -1), cotangent)
+    outs = pl.pallas_call(
+        hand_over,
+        out_shape=[jax.ShapeDtypeStruct(o.shape, o.dtype) for o in outs],
+        in_specs=[any_space] * 5,
+        out_specs=[any_space] * 5,
+        scratch_shapes=[pltpu.VMEM(o.shape, o.dtype) for o in outs]
+        + [pltpu.SemaphoreType.DMA((5,)), pltpu.SemaphoreType.DMA((5,))],
+    )(*outs)
     return (*outs[:4], outs[4].reshape(-1))
 
 

time: 49.3 us -> 40.7 us (0.83)
  local copies, waits for them, and re-layouts: 7.12 us -> 0 us
  Pallas kernels: 41.2 us -> 39.9 us
    unnamed x15 -> x0, local copies, waits for them, and re-layouts: 7.12 us -> none
    pallas_call x1, Pallas kernels: 41.2 us -> 38.2 us  [fused_body(): pl.pallas_call(fused_kernel, out_shape=[jax.ShapeDtypeStruct(query.shape,...]
    pallas_call x0 -> x1, Pallas kernels: none -> 1.73 us  [fused_body(): pl.pallas_call(hand_over, out_shape=[jax.ShapeDtypeStruct(o.shape, o.dtyp...]
where the time goes in v2:
time: 40.7 us; the launch traced here: 40.6 us
  Pallas kernels  39.9 us (98%)
  between operations  0.64 us (2%)
    pallas_call x1, Pallas kernels, fused_body(): pl.pallas_call(fused_kernel, out_shape=[jax.ShapeDtypeStruct(query.shape,...  38.2 us
    pallas_call x1, Pallas kernels, fused_body(): pl.pallas_call(hand_over, out_shape=[jax.ShapeDtypeStruct(o.shape, o.dtyp...  1.73 us

profile of v2, /device:TPU:0, one launch (start us, length us, event | category | flops | bytes accessed | tf_op | source)
XLA Modules:
  0.0 40.6 jit_solution(9194326868186481270)
XLA Ops:
  0.6 38.2 %shard_map.92 = (bf16[1,128,512]{2,1,0:T(8,128)(2,1)}, bf16[1,128,512]{2,1,0:T(8,128)(2,1)}, bf16[1,128,128]{2,1,0:T(8,128)(2,1)}, bf16[1,128,128]{2,1,0:T(8,128)(2,1)}, f32[1,512]{1,0:T(1,128)}) custom-call(bf16[1,128,512]{2,1,0:T(8,128)(2,1)} %q_ref.1, bf16[1,128,128]{2,1,0:T(8,128)(2,1)} %k_ref.1, bf16[1,128,128]{2,1,0:T(8,128)(2,1)} %v_ref.1, ...), custom_call_target="tpu_custom_call" | custom-call | flops 1610612736 | bytes 524288 | tf_op jit(solution)/shard_map/pallas_call | solution.py:424
  38.8 1.7 %shard_map.93 = (bf16[1,128,512]{2,1,0:T(8,128)(2,1)}, bf16[1,128,512]{2,1,0:T(8,128)(2,1)}, bf16[1,128,128]{2,1,0:T(8,128)(2,1)}, bf16[1,128,128]{2,1,0:T(8,128)(2,1)}, f32[1,512]{1,0:T(1,128)}) custom-call(bf16[1,128,512]{2,1,0:T(8,128)(2,1)} %get-tuple-element.15.refs_0_, bf16[1,128,512]{2,1,0:T(8,128)(2,1)} %get-tuple-element.16.refs_1_, ...), custom_call_target="tpu_custom_call" | custom-call | tf_op jit(solution)/shard_map/pallas_call | solution.py:445
